TPU v7x, 32 devices: a whole 2x2x4 slice. The times are simulated.
32 devices in a mesh: row: 4 (over y, x), col: 8 (over z, core).
Axes of the slice: x: 2, y: 2, z: 4, core: 2. Of those that a mesh axis runs over, the one named last changes fastest.
Arguments:
- amplitudes: float32 [128, 128, 6144], P('col', 'row'), may hold values from -6 to 6
- integrals: float32 [6144, 6144], P('col', 'row'), may hold values from -0.078125 to 0.078125
- amp_pattern: int32 [128, 48], P('col'), may hold values 0 or 1
- int_pattern: int32 [48, 48], P(None, 'row'), may hold values from 0 to 1
Outputs:
- ladder: float32 [128, 128, 6144], P('col', 'row')
All inputs are finite; a program needn't handle non-finite values. No bound on the sum of `amp_pattern` on one device may be relied on, other than what follows from the above.
Results may differ from a plain program's by a relative error of at most 0.00007.
Values sent between devices are 32-bit elements; how exact they have to be, the bound alone decides.
No kernel may reach another device: no remote copies, remote signals or barrier semaphores. Data moves between devices by JAX's collectives and lax.ppermute only.
A program may use at most 256 MiB of HBM per device.

v0:
```python
import jax
import jax.numpy as jnp
from jax import lax
from jax.sharding import PartitionSpec as P

TILE = 128


def expand_rows(pattern_f, start, count):
    positions = start + lax.broadcasted_iota(jnp.int32, (count, 1), 0)
    tile_ids = positions // TILE
    tile_range = lax.broadcasted_iota(jnp.int32, (count, pattern_f.shape[0]), 1)
    selector = (tile_ids == tile_range).astype(jnp.float32)
    return jnp.dot(
        selector, pattern_f, precision=lax.Precision.HIGHEST, preferred_element_type=jnp.float32
    )


def mask_integrals(piece, start, pattern_f):
    count = piece.shape[0]
    tiles_here = pattern_f.shape[1]
    row_mask = expand_rows(pattern_f, start, count)
    shaped = piece.reshape(count, tiles_here, TILE) * row_mask[:, :, None]
    return shaped.reshape(count, tiles_here * TILE)


def body(amplitudes, integrals, amp_pattern, int_pattern):
    first_local = amplitudes.shape[0]
    second_local = amplitudes.shape[1]
    depth = amplitudes.shape[2]
    ktiles = amp_pattern.shape[1]
    amp_mask = amp_pattern.astype(jnp.float32)
    int_mask = int_pattern.astype(jnp.float32)
    masked = (
        amplitudes.reshape(first_local, second_local, ktiles, TILE) * amp_mask[:, None, :, None]
    ).reshape(first_local, second_local, depth)
    gathered = lax.all_gather(integrals, "col", axis=0, tiled=True)
    weights = mask_integrals(gathered, 0, int_mask)
    product = jnp.einsum(
        "ijk,kn->ijn",
        lax.all_gather(masked, "row", axis=1, tiled=True),
        weights,
        precision=lax.Precision.HIGHEST,
        preferred_element_type=jnp.float32,
    )
    return lax.all_to_all(product, "row", split_axis=1, concat_axis=2, tiled=True)


def solution(mesh):
    placed = (P("col", "row", None), P("col", "row"), P("col", None), P(None, "row"))
    return jax.shard_map(
        body, mesh=mesh, in_specs=placed, out_specs=P("col", "row", None), check_vma=False
    )
```

profile of v0, /device:TPU:0, one launch (start us, length us, event | category | flops | bytes accessed | tf_op | source)
XLA Modules:
  0.0 1224.4 jit_solution(17242714788026242207)
XLA Ops:
  6.5 0.0 copy-start
  6.5 0.0 all-gather.5.cloned.1.call-start
  6.5 6.1 copy.14
  12.6 0.0 all-gather.5.cloned.1.call-update
  12.7 0.0 all-gather.3.cloned.1.call-start
  12.7 0.0 copy-done
  12.7 0.2 mul.24
  12.9 0.1 copy.22
  13.0 12.6 %broadcast_multiply_fusion = f32[16,32,6144]{2,1,0:T(8,128)} fusion(f32[16,32,6144]{2,1,0:T(8,128)} %param.4, f32[16,6144]{1,0:T(8,128)S(1)} %bitcast.15), kind=kLoop, calls=%fused_computation.3 | loop fusion | flops 3145728 | bytes 25559040 | tf_op jit(solution)/shard_map/mul | solution.py:35
  25.6 0.0 copy-start.1
  25.6 0.0 all-gather.3.cloned.1.call-update
  25.6 0.7 copy-done.1
  26.3 0.5 fusion.2
  26.8 313.3 %all-gather.5.cloned.1.call-done = f32[6144,1536]{0,1:T(8,128)} async-done(((f32[768,1536]{0,1:T(8,128)}), f32[6144,1536]{0,1:T(8,128)}) %all-gather.5.cloned.1.call-update) | async-done | bytes 37748752 | tf_op jit(solution)/shard_map/all_gather | solution.py:37
  340.0 32.3 %bitcast_multiply_fusion = f32[6144,1536]{0,1:T(8,128)} fusion(f32[6144,1536]{0,1:T(8,128)} %all-gather.5.cloned.1.call-done, f32[6144,12]{0,1:T(8,128)S(1)} %fusion.2), kind=kLoop, calls=%fused_computation.2 | loop fusion | flops 9437184 | bytes 75792384 | tf_op jit(solution)/shard_map/mul | solution.py:23
  372.4 406.3 %all-gather.3.cloned.1.call-done = f32[16,128,6144]{2,1,0:T(8,128)} async-done(((f32[16,32,6144]{2,1,0:T(8,128)}), f32[16,128,6144]{2,1,0:T(8,128)}) %all-gather.3.cloned.1.call-update) | async-done | bytes 50331664 | tf_op jit(solution)/shard_map/all_gather | solution.py:41
  778.7 250.4 %fusion = f32[16,128,1536]{2,1,0:T(8,128)} fusion(f32[16,128,6144]{2,1,0:T(8,128)} %all-gather.3.cloned.1.call-done, f32[6144,1536]{0,1:T(8,128)} %bitcast_multiply_fusion), kind=kOutput, calls=%fused_computation | convolution fusion | flops 231928233984 | bytes 100663296 | tf_op jit(solution)/shard_map/ijk,kn->ijn/dot_general | solution.py:39
  1029.0 16.4 %copy.16 = f32[16,128,1536]{2,0,1:T(8,128)} copy(f32[16,128,1536]{2,1,0:T(8,128)} %fusion) | data formatting | bytes 25165824 | tf_op jit(solution)/shard_map/ijk,kn->ijn/dot_general | solution.py:39
  1045.4 142.4 %all_to_all.18 = f32[16,128,1536]{2,0,1:T(8,128)S(1)} all-to-all(f32[16,128,1536]{2,0,1:T(8,128)} %copy.16), channel_id=1, replica_groups=mesh['row'=4,'col'=8] {'row'}, dimensions={1} | all-to-all | bytes 25165824 | tf_op jit(solution)/shard_map/all_to_all | solution.py:46
  1187.8 14.4 %copy.17 = f32[16,32,4,1536]{3,2,1,0:T(4,128)} copy(f32[16,32,4,1536]{3,0,1,2:T(8,128)S(1)} %bitcast.13) | data formatting | bytes 25165824 | tf_op jit(solution)/shard_map/all_to_all | solution.py:46
  1202.2 15.4 %all_to_all.16 = f32[16,32,6144]{2,1,0:T(8,128)} reshape(f32[16,32,4,1536]{3,2,1,0:T(4,128)} %copy.17) | data formatting | bytes 25165824 | tf_op jit(solution)/shard_map/all_to_all | solution.py:46
  (2 shorter events, 0.0 us)
Async XLA Ops:
  6.5 6.2 copy-start
  6.5 333.5 %all-gather.5.cloned.1.call-start = ((), (), s32[]{:S(2)}) async-start(), calls=%async_computation.2 | async-start | bytes 42467328 | tf_op jit(solution)/shard_map/all_gather | solution.py:37
  12.7 766.0 %all-gather.3.cloned.1.call-start = ((), (), s32[]{:S(2)}) async-start(), calls=%async_computation.1 | async-start | bytes 62914560 | tf_op jit(solution)/shard_map/all_gather | solution.py:41
  25.6 0.7 copy-start.1
Sparse Core Ops, SparseCore 0:
  12.8 327.2 all-gather.4
  341.9 436.7 all-gather.2
where the time goes:
time: 1230 us; the launch traced here: 1220 us
  waiting for transfers between devices  720 us (59%)
  matrix products  251 us (20%)
  blocking collectives  142 us (12%)
  local copies, waits for them, and re-layouts  53.2 us (4%)
  other arithmetic  44.9 us (4%)
  between operations  13.5 us (1%)
    all_gather x1, waiting for transfers between devices, body(): lax.all_gather(masked, 'row', axis=1, tiled=True)  406 us
    all_gather x1, waiting for transfers between devices, body(): gathered = lax.all_gather(integrals, 'col', axis=0, tiled=True)  313 us
    dot_general x1, matrix products, body(): jnp.einsum('ijk,kn->ijn', lax.all_gather(masked, 'row', axis=1, tiled=Tru...  250 us
    all_to_all x1, blocking collectives, body(): lax.all_to_all(product, 'row', split_axis=1, concat_axis=2, tiled=True)  142 us
    mul x1, other arithmetic, mask_integrals(): shaped = piece.reshape(count, tiles_here, TILE) * row_mask[:, :, None]  32.3 us
    all_to_all x2, local copies, waits for them, and re-layouts, body(): lax.all_to_all(product, 'row', split_axis=1, concat_axis=2, tiled=True)  29.8 us
  transfers between devices with their start and end apart: 2, of which 2 were waited for; matrix products, arithmetic and copies ran while one was open for 4% of the time, Pallas kernels for 0%

commit v1 on v0

v1 whole, which is shorter than its diff:
```python
import functools

import jax
import jax.numpy as jnp
from jax import lax
from jax.experimental import pallas as pl
from jax.experimental.pallas import tpu as pltpu
from jax.sharding import PartitionSpec as P

TILE = 128
CORES = 2
UNROLL = 3
VMEM_LIMIT = 48 * 1024 * 1024


def split_kernel(mine_pattern, other_pattern, mine_ref, other_ref, out_ref, *, second):
    k = pl.program_id(0)
    rows = mine_ref.shape[0]
    for half, (pattern, amp_ref) in enumerate(((mine_pattern, mine_ref), (other_pattern, other_ref))):
        for first in range(rows // second):
            value = amp_ref[pl.ds(first * second, second), :] * pattern[first, k].astype(jnp.float32)
            high = value.astype(jnp.bfloat16)
            low = (value - high.astype(jnp.float32)).astype(jnp.bfloat16)
            here = pl.ds(half * rows + first * second, second)
            out_ref[0, here, :TILE] = high
            out_ref[0, here, TILE:] = low


def split_amplitudes(mine, other, mine_pattern, other_pattern, second):
    rows, depth = mine.shape
    tiles = depth // TILE
    return pl.pallas_call(
        functools.partial(split_kernel, second=second),
        grid_spec=pltpu.PrefetchScalarGridSpec(
            num_scalar_prefetch=2,
            grid=(tiles,),
            in_specs=[pl.BlockSpec((rows, TILE), lambda k, *_: (0, k))] * 2,
            out_specs=pl.BlockSpec((1, CORES * rows, 2 * TILE), lambda k, *_: (k, 0, 0)),
        ),
        out_shape=jax.ShapeDtypeStruct((tiles, CORES * rows, 2 * TILE), jnp.bfloat16),
        compiler_params=pltpu.CompilerParams(vmem_limit_bytes=VMEM_LIMIT),
        cost_estimate=pl.CostEstimate(flops=8 * rows * depth, bytes_accessed=16 * rows * depth, transcendentals=0),
    )(mine_pattern, other_pattern, mine, other)


def pack_kernel(source_ref, row_ref, lane_ref, *refs, plan, sources):
    ins, outs = refs[:sources], refs[sources:]
    for out, (base, size) in zip(outs, plan):

        def copy(slot, _, out=out, base=base):
            row = pl.multiple_of(row_ref[base + slot], TILE)
            lane = pl.multiple_of(lane_ref[base + slot], TILE)
            for source in range(sources):

                @pl.when(source_ref[base + slot] == source)
                def _(source=source):
                    out[slot] = ins[source][pl.ds(row, TILE), pl.ds(lane, TILE)]

            return 0

        lax.fori_loop(0, size, copy, 0)


def pack(scalars, sources, plan):
    whole = lambda x: pl.BlockSpec(x.shape, lambda g, *s: (0,) * len(x.shape))
    outs = [jax.ShapeDtypeStruct((size, TILE, TILE), jnp.float32) for _, size in plan]
    return pl.pallas_call(
        functools.partial(pack_kernel, plan=plan, sources=len(sources)),
        grid_spec=pltpu.PrefetchScalarGridSpec(
            num_scalar_prefetch=len(scalars),
            grid=(1,),
            in_specs=[whole(x) for x in sources],
            out_specs=[whole(x) for x in outs],
        ),
        out_shape=outs,
        compiler_params=pltpu.CompilerParams(vmem_limit_bytes=VMEM_LIMIT),
        cost_estimate=pl.CostEstimate(
            flops=0, bytes_accessed=4 * (sum(x.size for x in sources) + sum(x.size for x in outs)), transcendentals=0
        ),
    )(*scalars, *sources)


def pool_kernel(sizes_ref, offsets_ref, *refs, segments):
    count = sum(len(parts) for parts in segments)
    ins, out, sem = refs[:count], refs[count], refs[count + 1]
    for waiting in (False, True):
        at = 0
        for e, parts in enumerate(segments):
            for a, b in parts:
                ref = ins[at]
                at += 1

                def step(slot, _, ref=ref, a=a, e=e):
                    place = offsets_ref[e] + slot
                    copy = pltpu.make_async_copy(ref.at[slot - a], out.at[place], sem.at[place])
                    if waiting:
                        copy.wait()
                    else:
                        copy.start()
                    return 0

                lax.fori_loop(a, jnp.maximum(a, jnp.minimum(b, sizes_ref[e])), step, 0)


def pool(sizes, offsets, pieces, capacity):
    arrays = [x for parts in pieces for x, _, _ in parts]
    segments = [[(a, b) for _, a, b in parts] for parts in pieces]
    return pl.pallas_call(
        functools.partial(pool_kernel, segments=segments),
        grid_spec=pltpu.PrefetchScalarGridSpec(
            num_scalar_prefetch=2,
            grid=(1,),
            in_specs=[pl.BlockSpec(memory_space=pl.ANY)] * len(arrays),
            out_specs=pl.BlockSpec(memory_space=pl.ANY),
            scratch_shapes=[pltpu.SemaphoreType.DMA((capacity,))],
        ),
        out_shape=jax.ShapeDtypeStruct((capacity, TILE, TILE), jnp.float32),
        compiler_params=pltpu.CompilerParams(vmem_limit_bytes=VMEM_LIMIT),
        cost_estimate=pl.CostEstimate(flops=0, bytes_accessed=8 * capacity * TILE * TILE, transcendentals=0),
    )(sizes, offsets, *arrays)


def gate_kernel(*refs):
    del refs


def gate(released, awaited):
    anywhere = pl.BlockSpec(memory_space=pl.ANY)
    return pl.pallas_call(
        gate_kernel,
        in_specs=[anywhere] * (len(released) + len(awaited)),
        out_specs=[anywhere] * len(released),
        out_shape=[jax.ShapeDtypeStruct(x.shape, x.dtype) for x in released],
        input_output_aliases={i: i for i in range(len(released))},
    )(*released, *awaited)


def multiply_kernel(
    plane_ref, low_ref, high_ref, shift_ref, base_ref, mine_at, other_at, fresh_ref, kk_ref, amp_ref, mine_in, other_in, *refs,
    segments, passed, steps, per_chip,
):
    count = len(segments)
    tiles = refs[:count]
    refs = refs[count + passed :]
    mine_ref, other_ref = refs[:2]
    buffer, sem = refs[2 + passed :]
    step = pl.program_id(0)
    rows = mine_ref.shape[0]

    def issue(g, half):
        low, high = low_ref[g], high_ref[g]
        for ref, (a, b, pooled, only) in zip(tiles, segments):
            shift = shift_ref[g] if pooled else -a

            def start(slot, _, ref=ref, shift=shift):
                pltpu.make_async_copy(
                    ref.at[slot + shift], buffer.at[half, slot - low], sem.at[half, slot - low]
                ).start()
                return 0

            first = jnp.maximum(low, a)
            last = jnp.maximum(first, jnp.minimum(high, b))
            if only is not None:
                last = jnp.where(g // per_chip == only, last, first)
            lax.fori_loop(first, last, start, 0)

    half = lax.rem(step, 2)

    @pl.when(step == 0)
    def _():
        issue(0, 0)

    @pl.when(step + 1 < steps)
    def _():
        issue(step + 1, 1 - half)

    @pl.when(fresh_ref[step] > 0)
    def _():
        mine_ref[...] = mine_in[...]
        other_ref[...] = other_in[...]

    low = low_ref[step]
    length = high_ref[step] - low
    base = base_ref[step] + low

    def wait(at, _):
        pltpu.make_async_copy(tiles[0].at[0], buffer.at[half, at], sem.at[half, at]).wait()
        return 0

    lax.fori_loop(0, length, wait, 0)

    def add(turn, _):
        weights, ks = [], []
        for u in range(UNROLL):
            at = turn * UNROLL + u
            inside = at < length
            at = jnp.minimum(at, length - 1)
            value = buffer[half, at]
            if u:
                value = jnp.where(inside, value, 0.0)
            high = value.astype(jnp.bfloat16)
            rest = (value - high.astype(jnp.float32)).astype(jnp.bfloat16)
            weights.append(jnp.concatenate([high, rest], axis=1))
            weights.append(jnp.concatenate([high, jnp.zeros_like(high)], axis=1))
            ks.append(kk_ref[base + at])
        left = jnp.concatenate([amp_ref[k] for k in ks], axis=1)
        product = jnp.dot(left, jnp.concatenate(weights, axis=0), preferred_element_type=jnp.float32)
        total = product[:, :TILE] + product[:, TILE:]
        mine_ref[...] += total[:rows]
        other_ref[...] += total[rows:]
        return 0

    lax.fori_loop(0, (length + UNROLL - 1) // UNROLL, add, 0)


def multiply(scalars, steps, per_chip, amps, mine, other, pieces, kd, released=()):
    rows = mine.shape[0]
    segments = [piece[1:] for piece in pieces]
    expected = 10 * steps
    n = len(scalars)
    mine_spec = pl.BlockSpec((rows, TILE), lambda g, *s: (0, s[5][g]))
    other_spec = pl.BlockSpec((rows, TILE), lambda g, *s: (0, s[6][g]))
    anywhere = pl.BlockSpec(memory_space=pl.ANY)
    first = n + 3 + len(pieces)
    aliases = {n + 1: 0, n + 2: 1}
    aliases.update({first + i: 2 + i for i in range(len(released))})
    return pl.pallas_call(
        functools.partial(multiply_kernel, segments=segments, passed=len(released), steps=steps, per_chip=per_chip),
        grid_spec=pltpu.PrefetchScalarGridSpec(
            num_scalar_prefetch=n,
            grid=(steps,),
            in_specs=[
                pl.BlockSpec((CORES * kd, CORES * rows, 2 * TILE), lambda g, *s: (s[0][0], 0, 0)),
                mine_spec,
                other_spec,
            ]
            + [anywhere] * (len(pieces) + len(released)),
            out_specs=[mine_spec, other_spec] + [anywhere] * len(released),
            scratch_shapes=[
                pltpu.VMEM((2, CORES * kd, TILE, TILE), jnp.float32),
                pltpu.SemaphoreType.DMA((2, CORES * kd)),
            ],
        ),
        out_shape=[jax.ShapeDtypeStruct(x.shape, x.dtype) for x in (mine, other, *released)],
        input_output_aliases=aliases,
        compiler_params=pltpu.CompilerParams(vmem_limit_bytes=VMEM_LIMIT),
        cost_estimate=pl.CostEstimate(
            flops=expected * 32 * rows * TILE * TILE,
            bytes_accessed=expected * 4 * TILE * TILE,
            transcendentals=0,
        ),
    )(*scalars, amps, mine, other, *[piece[0] for piece in pieces], *released)


def place_kernel(at_ref, mine_in, piece_ref, out_ref):
    out_ref[...] = mine_in[...] + piece_ref[...]


def place(at, mine, piece):
    rows = mine.shape[0]
    spec = pl.BlockSpec((rows, TILE), lambda g, a: (0, a[g]))
    return pl.pallas_call(
        place_kernel,
        grid_spec=pltpu.PrefetchScalarGridSpec(
            num_scalar_prefetch=1,
            grid=(at.shape[0],),
            in_specs=[spec, pl.BlockSpec((rows, TILE), lambda g, a: (0, g))],
            out_specs=spec,
        ),
        out_shape=jax.ShapeDtypeStruct(mine.shape, mine.dtype),
        input_output_aliases={1: 0},
        compiler_params=pltpu.CompilerParams(vmem_limit_bytes=VMEM_LIMIT),
        cost_estimate=pl.CostEstimate(flops=piece.size, bytes_accessed=12 * piece.size, transcendentals=0),
    )(at, mine, piece)


def body(amplitudes, integrals, amp_pattern, int_pattern, *, chips, devices):
    R, Z = chips, devices // CORES
    first, second, depth = amplitudes.shape
    rows = first * second
    kd = integrals.shape[0] // TILE
    ntl = integrals.shape[1] // TILE
    groups = R if ntl % R == 0 else 1
    width = ntl // groups
    per_chip = -(-ntl // CORES)
    tiles = per_chip * CORES * kd

    r = lax.axis_index("row")
    col = lax.axis_index("col")
    core = lax.rem(col, CORES)
    ring = [0] + list(range(1, Z, 2)) + [z for z in range(Z - 1, 0, -1) if z % 2 == 0]
    spot = [ring.index(z) for z in range(Z)]

    def by_row(x, distance):
        return lax.ppermute(x, "row", [(a, a ^ distance) for a in range(R)])

    def by_core(x):
        return lax.ppermute(x, "col", [(a, a ^ 1) for a in range(Z * CORES)])

    def by_plane(x):
        return lax.ppermute(
            x,
            "col",
            [(ring[a] * CORES + c, ring[(a + 1) % Z] * CORES + c) for a in range(Z) for c in range(CORES)],
        )

    shares = [integrals[:, : width * TILE] if groups > 1 else integrals]
    for d in range(1, groups):
        shares.append(by_row(integrals[:, d * width * TILE : (d + 1) * width * TILE], d))

    amps_mine = amplitudes.reshape(rows, depth)
    amps = split_amplitudes(amps_mine, by_core(amps_mine), amp_pattern, by_core(amp_pattern), second)
    mine = jnp.zeros((rows, (R * ntl + per_chip * CORES - ntl) * TILE), jnp.float32)
    if groups > 1:
        *shares[1:], mine = gate([*shares[1:], mine], [amps])
    twins = [by_core(x) for x in shares]

    patterns = [int_pattern] + [by_row(int_pattern, d) for d in range(1, R)]
    by_distance = jnp.stack(patterns).reshape(R, Z, CORES * kd, groups, width)
    near = []
    for e in range(R):
        picked = jnp.stack([by_distance[e ^ d, :, :, d] for d in range(groups)], axis=2)
        near.append(picked.reshape(Z, CORES * kd, ntl))
    present = (jnp.stack(near, axis=1) != 0).astype(jnp.int32)
    present = jnp.pad(present, ((0, 0), (0, 0), (0, 0), (0, per_chip * CORES - ntl)))
    present = present.reshape(Z, R, CORES * kd, per_chip, CORES).transpose(0, 1, 4, 3, 2)
    both = present.reshape(Z, R, CORES, tiles)
    cores_counts = jnp.sum(both, axis=-1)
    own = jnp.where(core == 0, both[:, :, 0], both[:, :, 1])
    here = jnp.asarray(spot)[col // CORES]
    planes = jnp.asarray(ring)[lax.rem(here - jnp.arange(Z) + Z, Z)]
    if R == 4:
        own = jnp.stack(
            [
                own[:, 0],
                jnp.where(core == 0, own[:, 1], own[:, 2]),
                jnp.where(core == 0, own[:, 2], own[:, 1]),
                own[:, 3],
            ],
            axis=1,
        )
    own = own[planes]
    counts = jnp.sum(own, axis=-1)
    ids = jnp.arange(tiles)
    slot_of = jnp.sum(own[..., None, :] * (ids[None, :] < ids[:, None]), axis=-1)
    slots = (
        jnp.sum(
            (ids + 1)[None, None, None, :]
            * ((slot_of[:, :, None, :] == ids[:, None]) & (own[:, :, None, :] > 0)),
            axis=-1,
        )
        - 1
    )
    ends = jnp.sum(own[:, :, None, :] * (ids[None, :] < (jnp.arange(per_chip + 1) * CORES * kd)[:, None]), axis=-1)

    straight = max(2, round(tiles * 35 / 72)) if R == 4 else max(4, 2 * round(tiles * 25 / 72))
    extra = max(2, round(tiles * 16 / 72)) if R == 4 else 0
    pooled = max(R, round(tiles * 32 / 72)) if R == 4 else 0
    longest = tiles + straight + extra
    slots = jnp.pad(slots, ((0, 0), (0, 0), (0, longest - tiles)), constant_values=-1)
    most = jnp.max(cores_counts)

    def chips_of(which):
        return r ^ (jnp.stack([0 * which, 1 + which, 2 - which, 0 * which + 3]) if R == 4 else jnp.arange(R))

    chip_of = chips_of(core)
    blocks = R * ntl
    spare = per_chip * CORES - ntl

    def columns_of(which):
        column = jnp.arange(per_chip)[None, :] * CORES + which
        group = column // width
        chip = chips_of(which)[:, None]
        at = (((chip ^ group) if groups > 1 else chip) * groups + group) * width + column % width
        return jnp.where(column < ntl, at, blocks).astype(jnp.int32)

    mine_at = columns_of(core)
    received_at = columns_of(1 - core)

    def across(x, near):
        return lax.ppermute(
            x,
            ("row", "col"),
            [
                (a * devices + d, (a ^ (near if d % CORES == 0 else 3 - near)) * devices + d)
                for a in range(R)
                for d in range(devices)
            ],
        )

    def one_round(state):
        base, mine = state
        after = base + straight
        left = jnp.clip(cores_counts - after, 0, extra)
        fits = jnp.max(jnp.sum(left, axis=1)) <= pooled
        taken = jnp.where(fits, extra, pooled // R) if extra else jnp.int32(0)
        sizes = jnp.clip(counts - after, 0, taken)
        before = chip_of[None, :] < chip_of[:, None]
        offsets = jnp.sum(sizes[:, None, :] * before[None], axis=-1).astype(jnp.int32)
        now = lax.dynamic_slice_in_dim(slots, base, straight + extra, axis=2)
        kk = jnp.maximum(now, 0) % (CORES * kd)
        bounds = jnp.clip(ends - base, 0, straight + taken).astype(jnp.int32)

        column = now[0, 0] // (CORES * kd) * CORES + core
        holder = kk[0, 0] // kd
        source = jnp.where(now[0, 0] < 0, -1, (holder != core) * groups + column // width)
        where = [source, kk[0, 0] % kd * TILE, column % width * TILE]
        plan = ((0, straight), (straight, extra), (0, straight)) if extra else ((0, straight),)
        packed = pack([x.astype(jnp.int32) for x in where], shares + twins, plan)

        other = jnp.zeros((rows, R * per_chip * TILE), jnp.float32)

        def add(mine, other, step, neighbours, low_slot, high_slot, pieces, released=(), sparse=False):
            low, high, shift, base_at = [], [], [], []
            for e in neighbours:
                limits = jnp.clip(bounds[step, e], low_slot, high_slot)
                low.append(limits[:-1])
                high.append(limits[1:])
                shift.append(jnp.broadcast_to(offsets[step, e] - straight, (per_chip,)))
                base_at.append(jnp.full((per_chip,), (e - neighbours[0]) * (straight + extra)))
            first_e, last_e = neighbours[0], neighbours[-1] + 1
            lists = [jnp.concatenate(x) for x in (low, high, shift, base_at)]
            lists.append(mine_at[first_e:last_e].reshape(-1))
            lists.append(jnp.arange(first_e * per_chip, last_e * per_chip))
            steps = len(neighbours) * per_chip
            if sparse:
                full = lists[1] > lists[0]
                ids = jnp.arange(steps)
                spots = jnp.sum(full[None, :] & (ids[None, :] < ids[:, None]), axis=1)
                taken_spot = jnp.minimum(ids, jnp.maximum(jnp.sum(full) - 1, 0))
                chosen = (spots[None, :] == taken_spot[:, None]) & full[None, :]
                lists = [jnp.sum(jnp.where(chosen, x[None, :], 0), axis=1) for x in lists]
                fresh = (ids == 0) | (ids < jnp.sum(full))
                lists[1] = jnp.where(fresh, lists[1], lists[0])
            else:
                fresh = jnp.ones((steps,), jnp.int32)
            lists.append(fresh)
            scalars = [planes[step].reshape(1), *lists, kk[step, first_e:last_e].reshape(-1)]
            scalars = [x.astype(jnp.int32) for x in scalars]
            return multiply(scalars, steps, per_chip, amps, mine, other, pieces, kd, released)

        if R == 4:
            end = straight + extra
            sent, late = packed[0], packed[1]
            along = [sent, by_plane(sent)]
            first_late, second_late = across(late, 1), across(late, 2)
            at_home = [(sent, 0, straight, False, None), (late, straight, end, False, None)]
            mine, other = add(mine, other, 0, [0], 0, end, at_home)
            third_late = across(first_late, 2)
            spare_sent, mine = gate([packed[2], mine], [third_late])
            first_near, second_near = across(spare_sent, 1), across(spare_sent, 2)
            pools = [
                pool(
                    sizes[0].astype(jnp.int32),
                    offsets[0],
                    [[(x, 0, extra)] for x in (late, first_late, second_late, third_late)],
                    pooled,
                )
            ]
            pools.append(by_plane(pools[0]))
            block = per_chip * TILE
            received = []
            for step in range(Z):
                mixed = (pools[step], straight, end, True, None)
                if step:
                    mine, other = add(mine, other, step, [0], 0, end, [(along[step], 0, straight, False, None), mixed])
                if step == Z - 1:
                    received.append(by_core(other[:, :block]))
                third_near = across(first_near, 2)
                near = [(first_near, 0, straight, False, 0), (second_near, 0, straight, False, 1), mixed]
                if step + 1 < Z:
                    along[step + 1], mine = gate([along[step + 1], mine], [first_near, second_near])
                    first_near, second_near = across(along[step + 1], 1), across(along[step + 1], 2)
                    if step + 2 < Z:
                        along.append(by_plane(along[step + 1]))
                        pools.append(by_plane(pools[step + 1]))
                mine, other = add(mine, other, step, [1, 2], 0, end, near)
                if step == Z - 1:
                    received.append(by_core(other[:, block : 3 * block]))
                    mine = place(received_at[0], mine, received[0])
                mine, other = add(mine, other, step, [3], 0, end, [(third_near, 0, straight, False, None), mixed])
            received.append(by_core(other[:, 3 * block :]))
            mine = place(received_at[1:3].reshape(-1), mine, received[1])
            mine = place(received_at[3], mine, received[2])
        else:
            now_at = packed[0]
            for step in range(Z):
                for e in range(R):
                    piece = by_row(now_at, e) if e else now_at
                    mine, other = add(mine, other, step, [e], 0, straight, [(piece, 0, straight, False, None)])
                if step + 1 < Z:
                    now_at = by_plane(now_at)
            mine = place(received_at.reshape(-1), mine, by_core(other))
        return base + straight + taken, mine

    state = one_round((jnp.int32(0), mine))
    _, mine = lax.while_loop(lambda state: state[0] < most, one_round, state)
    return mine[:, : blocks * TILE].reshape(first, second, blocks * TILE)


def solution(mesh):
    placed = (P("col", "row", None), P("col", "row"), P("col", None), P(None, "row"))
    return jax.shard_map(
        functools.partial(body, chips=mesh.shape["row"], devices=mesh.shape["col"]),
        mesh=mesh,
        in_specs=placed,
        out_specs=P("col", "row", None),
        check_vma=False,
    )
```

time: 1230 us -> 609 us (0.50)
  waiting for transfers between devices: 720 us -> 137 us
  Pallas kernels: 0 us -> 349 us
  matrix products: 251 us -> 0 us
  blocking collectives: 142 us -> 0 us
  starting transfers between devices: 0.04 us -> 48.1 us
  other arithmetic: 44.9 us -> 5.73 us
    all_gather x2 -> x0, waiting for transfers between devices: 720 us -> none  [the longest x1 406 us: body(): lax.all_gather(masked, 'row', axis=1, tiled=True)]
    pallas_call x0 -> x23, Pallas kernels: none -> 349 us  [the longest x12 259 us: multiply(): pl.pallas_call(functools.partial(multiply_kernel, segments=segments, pass...]
    dot_general x2 -> x0, matrix products: 251 us -> none  [the longest x1 250 us: body(): jnp.einsum('ijk,kn->ijn', lax.all_gather(masked, 'row', axis=1, tiled=Tru...]
    all_to_all x1 -> x0, blocking collectives: 142 us -> none  [body(): lax.all_to_all(product, 'row', split_axis=1, concat_axis=2, tiled=True)]
    ppermute x0 -> x36, waiting for transfers between devices: none -> 137 us  [the longest x6 62.8 us: by_plane(): lax.ppermute(x, 'col', [(ring[a] * CORES + c, ring[(a + 1) % Z] * CORES +...]
    ppermute x0 -> x36, starting transfers between devices: none -> 48.1 us  [the longest x15 27.6 us: across(): lax.ppermute(x, ('row', 'col'), [(a * devices + d, (a ^ (near if d % CORE...]
    mul x2 -> x3, other arithmetic: 44.9 us -> 0.05 us  [the longest x2 0.04 us: one_round(): where = [source, kk[0, 0] % kd * TILE, column % width * TILE]]
    all_to_all x2 -> x0, local copies, waits for them, and re-layouts: 29.8 us -> none  [body(): lax.all_to_all(product, 'row', split_axis=1, concat_axis=2, tiled=True)]
  transfers between devices with their start and end apart: 2 -> 36, of which waited for: 2 -> 12; matrix products, arithmetic and copies ran while one was open for 4% -> 6% of each run, Pallas kernels for 0% -> 55%
where the time goes in v1:
time: 609 us; the launch traced here: 601 us
  Pallas kernels  349 us (57%)
  waiting for transfers between devices  137 us (22%)
  local copies, waits for them, and re-layouts  49 us (8%)
  starting transfers between devices  48.1 us (8%)
  between operations  11.4 us (2%)
    pallas_call x12, Pallas kernels, multiply(): pl.pallas_call(functools.partial(multiply_kernel, segments=segments, pass...  259 us
    ppermute x6, waiting for transfers between devices, by_plane(): lax.ppermute(x, 'col', [(ring[a] * CORES + c, ring[(a + 1) % Z] * CORES +...  62.8 us
    ppermute x15, waiting for transfers between devices, across(): lax.ppermute(x, ('row', 'col'), [(a * devices + d, (a ^ (near if d % CORE...  59.1 us
    pallas_call x1, Pallas kernels, split_amplitudes(): pl.pallas_call(functools.partial(split_kernel, second=second), grid_spec=...  35.2 us
    ppermute x15, starting transfers between devices, across(): lax.ppermute(x, ('row', 'col'), [(a * devices + d, (a ^ (near if d % CORE...  27.6 us
    pallas_call x1, Pallas kernels, pool(): pl.pallas_call(functools.partial(pool_kernel, segments=segments), grid_sp...  23.8 us
    pallas_call x3, Pallas kernels, place(): pl.pallas_call(place_kernel, grid_spec=pltpu.PrefetchScalarGridSpec(num_s...  19.2 us
    unnamed x86, local copies, waits for them, and re-layouts  18.2 us
  transfers between devices with their start and end apart: 36, of which 12 were waited for; matrix products, arithmetic and copies ran while one was open for 6% of the time, Pallas kernels for 55%

profile of v1, /device:TPU:0, one launch (start us, length us, event | category | flops | bytes accessed | tf_op | source)
XLA Modules:
  0.0 601.1 jit_solution(14448904276921179238)
XLA Ops:
  24.0 35.2 %shard_map.64.refs_4_.amp_ref = bf16[48,1024,256]{2,1,0:T(8,128)(2,1)} custom-call(s32[16,48]{1,0:T(8,128)S(1)} %copy-done.31, s32[16,48]{1,0:T(8,128)S(1)} %collective-permute-done.27.other_pattern, f32[512,6144]{1,0:T(8,128)} %bitcast.311, f32[512,6144]{1,0:T(8,128)} %collective-permute-done.28.other_ref), custom_call_target="tpu_custom_call" | custom-call | flops 25165824 | bytes 50331648 | tf_op jit(solution)/shard_map/pallas_call | solution.py:32
  59.2 9.9 %collective-permute-done.30.refs_1_ = f32[768,384]{1,0:T(8,128)} collective-permute-done((f32[768,384]{1,0:T(8,128)}, f32[768,384]{1,0:T(8,128)}, u32[]{:S(2)}, u32[]{:S(2)}) %collective-permute-start.30) | collective-permute-done | bytes 1179680 | tf_op jit(solution)/shard_map/ppermute | solution.py:295
  69.1 6.3 %broadcast_in_dim.163.refs_3_ = f32[512,6144]{1,0:T(8,128)} broadcast(f32[]{:T(128)} %constant.389.clone.1), dimensions={} | broadcast | bytes 12582916 | tf_op jit(solution)/shard_map/broadcast_in_dim | solution.py:313
  82.0 11.9 %shard_map.66 = (f32[35,128,128]{2,1,0:T(8,128)}, f32[16,128,128]{2,1,0:T(8,128)}, f32[35,128,128]{2,1,0:T(8,128)S(1)}) custom-call(s32[51]{0:T(128)S(1)} %get-tuple-element.793.source_ref, s32[51]{0:T(128)S(1)} %get-tuple-element.792.row_ref, s32[51]{0:T(128)S(1)} %get-tuple-element.644.lane_ref, f32[768,384]{1,0:T(8,128)S(1)} %get-tuple-element.1220.refs_0_, ...), custom_call_target="tpu_custom_call" | custom-call | bytes 15073280 | tf_op jit(solution)/shard_map/pallas_call | solution.py:67
  100.0 20.0 %collective-permute-done.37.refs_1_ = f32[16,128,128]{2,1,0:T(8,128)S(1)} collective-permute-done((f32[16,128,128]{2,1,0:T(8,128)}, f32[16,128,128]{2,1,0:T(8,128)S(1)}, u32[]{:S(2)}, u32[]{:S(2)}) %collective-permute-start.37) | collective-permute-done | bytes 1048608 | tf_op jit(solution)/shard_map/ppermute | solution.py:381
  126.2 16.1 %shard_map.67 = (f32[512,6144]{1,0:T(8,128)}, f32[512,3072]{1,0:T(8,128)}) custom-call(s32[1]{0:T(128)} %get-tuple-element.819.plane_ref, s32[6]{0:T(128)S(1)} %get-tuple-element.585.low_ref, s32[6]{0:T(128)S(1)} %get-tuple-element.584.high_ref, s32[6]{0:T(128)S(1)} %broadcast_in_dim.164.shift_ref, ...), custom_call_target="tpu_custom_call", output_to_operand_aliasing={{0}: (10, {}), {1}: (11, {})} | custom-call | flops 16106127360 | bytes 3932160 | tf_op jit(solution)/shard_map/pallas_call | solution.py:227
  156.8 23.8 %shard_map.70.refs_2_.refs_1_ = f32[32,128,128]{2,1,0:T(8,128)} custom-call(s32[4]{0:T(128)S(1)} %slice_bitcast_fusion.71.sizes_ref, s32[4]{0:T(128)S(1)} %slice_bitcast_fusion.70.offsets_ref, f32[16,128,128]{2,1,0:T(8,128)} %get-tuple-element.427.refs_1_.refs_0_, f32[16,128,128]{2,1,0:T(8,128)S(1)} %copy-done.30, ...), custom_call_target="tpu_custom_call" | custom-call | bytes 4194304 | tf_op jit(solution)/shard_map/pallas_call | solution.py:108
  183.0 40.9 %collective-permute-done.44.refs_1_.refs_2_ = f32[32,128,128]{2,1,0:T(8,128)} collective-permute-done((f32[32,128,128]{2,1,0:T(8,128)}, f32[32,128,128]{2,1,0:T(8,128)}, u32[]{:S(2)}, u32[]{:S(2)}) %collective-permute-start.44) | collective-permute-done | bytes 2097184 | tf_op jit(solution)/shard_map/ppermute | solution.py:301
  227.8 6.1 %collective-permute-start.45 = (f32[35,128,128]{2,1,0:T(8,128)}, f32[35,128,128]{2,1,0:T(8,128)S(1)}, u32[]{:S(2)}, u32[]{:S(2)}) collective-permute-start(f32[35,128,128]{2,1,0:T(8,128)} %get-tuple-element.431.refs_0_), channel_id=1, source_target_pairs={{0,8},{1,17},{2,10},{3,19},{4,12},{5,21},{6,14},{7,23},{8,0},{9,25... | collective-permute-start | bytes 6881288 | tf_op jit(solution)/shard_map/ppermute | solution.py:381
  240.3 29.4 %shard_map.71 = (f32[512,6144]{1,0:T(8,128)}, f32[512,3072]{1,0:T(8,128)}) custom-call(s32[1]{0:T(128)} %get-tuple-element.819.plane_ref, s32[12]{0:T(128)S(1)} %pad_add_fusion.21.low_ref, s32[12]{0:T(128)S(1)} %pad_add_fusion.22.high_ref, s32[12]{0:T(128)S(1)} %concatenate.94.shift_ref, ...), custom_call_target="tpu_custom_call", output_to_operand_aliasing={{0}: (10, {}), {1}: (11, {})} | custom-call | flops 32212254720 | bytes 7864320 | tf_op jit(solution)/shard_map/pallas_call | solution.py:227
  275.4 17.8 %shard_map.72 = (f32[512,6144]{1,0:T(8,128)}, f32[512,3072]{1,0:T(8,128)}) custom-call(s32[1]{0:T(128)} %get-tuple-element.819.plane_ref, s32[6]{0:T(128)S(1)} %get-tuple-element.581.low_ref, s32[6]{0:T(128)S(1)} %get-tuple-element.580.high_ref, s32[6]{0:T(128)S(1)} %broadcast_in_dim.166.shift_ref, ...), custom_call_target="tpu_custom_call", output_to_operand_aliasing={{0}: (10, {}), {1}: (11, {})} | custom-call | flops 16106127360 | bytes 3932160 | tf_op jit(solution)/shard_map/pallas_call | solution.py:227
  293.2 17.8 %shard_map.73 = (f32[512,6144]{1,0:T(8,128)}, f32[512,3072]{1,0:T(8,128)}) custom-call(s32[1]{0:T(128)} %get-tuple-element.818.plane_ref, s32[6]{0:T(128)S(1)} %get-tuple-element.583.low_ref, s32[6]{0:T(128)S(1)} %get-tuple-element.582.high_ref, s32[6]{0:T(128)S(1)} %broadcast_in_dim.165.shift_ref, ...), custom_call_target="tpu_custom_call", output_to_operand_aliasing={{0}: (10, {}), {1}: (11, {})} | custom-call | flops 16106127360 | bytes 3932160 | tf_op jit(solution)/shard_map/pallas_call | solution.py:227
  311.0 11.8 %collective-permute-done.41.refs_0_ = f32[35,128,128]{2,1,0:T(8,128)S(1)} collective-permute-done((f32[35,128,128]{2,1,0:T(8,128)}, f32[35,128,128]{2,1,0:T(8,128)S(1)}, u32[]{:S(2)}, u32[]{:S(2)}) %collective-permute-start.41) | collective-permute-done | bytes 2293792 | tf_op jit(solution)/shard_map/ppermute | solution.py:301
  337.3 30.9 %shard_map.75 = (f32[512,6144]{1,0:T(8,128)}, f32[512,3072]{1,0:T(8,128)}) custom-call(s32[1]{0:T(128)} %get-tuple-element.818.plane_ref, s32[12]{0:T(128)S(1)} %pad_add_fusion.23.low_ref, s32[12]{0:T(128)S(1)} %pad_add_fusion.24.high_ref, s32[12]{0:T(128)S(1)} %concatenate.97.shift_ref, ...), custom_call_target="tpu_custom_call", output_to_operand_aliasing={{0}: (10, {}), {1}: (11, {})} | custom-call | flops 32212254720 | bytes 7864320 | tf_op jit(solution)/shard_map/pallas_call | solution.py:227
  368.6 18.4 %shard_map.76 = (f32[512,6144]{1,0:T(8,128)}, f32[512,3072]{1,0:T(8,128)}) custom-call(s32[1]{0:T(128)} %get-tuple-element.818.plane_ref, s32[6]{0:T(128)S(1)} %get-tuple-element.573.low_ref, s32[6]{0:T(128)S(1)} %get-tuple-element.572.high_ref, s32[6]{0:T(128)S(1)} %broadcast_in_dim.169.shift_ref, ...), custom_call_target="tpu_custom_call", output_to_operand_aliasing={{0}: (10, {}), {1}: (11, {})} | custom-call | flops 16106127360 | bytes 3932160 | tf_op jit(solution)/shard_map/pallas_call | solution.py:227
  387.1 17.4 %shard_map.77 = (f32[512,6144]{1,0:T(8,128)}, f32[512,3072]{1,0:T(8,128)}) custom-call(s32[1]{0:T(128)} %get-tuple-element.820.plane_ref, s32[6]{0:T(128)S(1)} %get-tuple-element.575.low_ref, s32[6]{0:T(128)S(1)} %get-tuple-element.574.high_ref, s32[6]{0:T(128)S(1)} %broadcast_in_dim.168.shift_ref, ...), custom_call_target="tpu_custom_call", output_to_operand_aliasing={{0}: (10, {}), {1}: (11, {})} | custom-call | flops 16106127360 | bytes 3932160 | tf_op jit(solution)/shard_map/pallas_call | solution.py:227
  404.5 6.0 collective-permute-done.47.refs_0_
  417.0 30.0 %shard_map.79 = (f32[512,6144]{1,0:T(8,128)}, f32[512,3072]{1,0:T(8,128)}) custom-call(s32[1]{0:T(128)} %get-tuple-element.820.plane_ref, s32[12]{0:T(128)S(1)} %pad_add_fusion.19.low_ref, s32[12]{0:T(128)S(1)} %pad_add_fusion.20.high_ref, s32[12]{0:T(128)S(1)} %concatenate.91.shift_ref, ...), custom_call_target="tpu_custom_call", output_to_operand_aliasing={{0}: (10, {}), {1}: (11, {})} | custom-call | flops 32212254720 | bytes 7864320 | tf_op jit(solution)/shard_map/pallas_call | solution.py:227
  447.0 38.8 %collective-permute-done.52.refs_0_ = f32[35,128,128]{2,1,0:T(8,128)S(1)} collective-permute-done((f32[35,128,128]{2,1,0:T(8,128)}, f32[35,128,128]{2,1,0:T(8,128)S(1)}, u32[]{:S(2)}, u32[]{:S(2)}) %collective-permute-start.52) | collective-permute-done | bytes 2293792 | tf_op jit(solution)/shard_map/ppermute | solution.py:381
  485.8 18.4 %shard_map.80 = (f32[512,6144]{1,0:T(8,128)}, f32[512,3072]{1,0:T(8,128)}) custom-call(s32[1]{0:T(128)} %get-tuple-element.820.plane_ref, s32[6]{0:T(128)S(1)} %get-tuple-element.591.low_ref, s32[6]{0:T(128)S(1)} %get-tuple-element.590.high_ref, s32[6]{0:T(128)S(1)} %broadcast_in_dim.160.shift_ref, ...), custom_call_target="tpu_custom_call", output_to_operand_aliasing={{0}: (10, {}), {1}: (11, {})} | custom-call | flops 16106127360 | bytes 3932160 | tf_op jit(solution)/shard_map/pallas_call | solution.py:227
  504.3 17.1 %shard_map.81 = (f32[512,6144]{1,0:T(8,128)}, f32[512,3072]{1,0:T(8,128)}) custom-call(s32[1]{0:T(128)} %get-tuple-element.821.plane_ref, s32[6]{0:T(128)S(1)} %get-tuple-element.593.low_ref, s32[6]{0:T(128)S(1)} %get-tuple-element.592.high_ref, s32[6]{0:T(128)S(1)} %broadcast_in_dim.159.shift_ref, ...), custom_call_target="tpu_custom_call", output_to_operand_aliasing={{0}: (10, {}), {1}: (11, {})} | custom-call | flops 16106127360 | bytes 3932160 | tf_op jit(solution)/shard_map/pallas_call | solution.py:227
  527.1 27.6 %shard_map.82 = (f32[512,6144]{1,0:T(8,128)}, f32[512,3072]{1,0:T(8,128)}) custom-call(s32[1]{0:T(128)} %get-tuple-element.821.plane_ref, s32[12]{0:T(128)S(1)} %pad_add_fusion.17.low_ref, s32[12]{0:T(128)S(1)} %pad_add_fusion.18.high_ref, s32[12]{0:T(128)S(1)} %concatenate.88.shift_ref, ...), custom_call_target="tpu_custom_call", output_to_operand_aliasing={{0}: (10, {}), {1}: (11, {})} | custom-call | flops 32212254720 | bytes 7864320 | tf_op jit(solution)/shard_map/pallas_call | solution.py:227
  565.3 17.8 %shard_map.84 = (f32[512,6144]{1,0:T(8,128)}, f32[512,3072]{1,0:T(8,128)}) custom-call(s32[1]{0:T(128)} %get-tuple-element.821.plane_ref, s32[6]{0:T(128)S(1)} %get-tuple-element.599.low_ref, s32[6]{0:T(128)S(1)} %get-tuple-element.598.high_ref, s32[6]{0:T(128)S(1)} %broadcast_in_dim.156.shift_ref, ...), custom_call_target="tpu_custom_call", output_to_operand_aliasing={{0}: (10, {}), {1}: (11, {})} | custom-call | flops 16106127360 | bytes 3932160 | tf_op jit(solution)/shard_map/pallas_call | solution.py:227
  586.2 8.5 %shard_map.85.mine_in = f32[512,6144]{1,0:T(8,128)} custom-call(s32[12]{0:T(128)S(1)} %reshape.642.at_ref, f32[512,6144]{1,0:T(8,128)} %get-tuple-element.458.mine_in, f32[512,1536]{1,0:T(8,128)S(1)} %collective-permute-done.58.piece_ref), custom_call_target="tpu_custom_call", output_to_operand_aliasing={{}: (1, {})} | custom-call | flops 786432 | bytes 9437184 | tf_op jit(solution)/shard_map/pallas_call | solution.py:262
  (283 shorter events, 111.7 us)
Async XLA Ops:
  14.2 45.0 %collective-permute-start.29 = (f32[768,384]{1,0:T(8,128)}, f32[768,384]{1,0:T(8,128)S(1)}, u32[]{:S(2)}, u32[]{:S(2)}) collective-permute-start(f32[768,384]{1,0:T(8,128)} %get-tuple-element.745), channel_id=1, source_target_pairs={{0,8},{8,0},{16,24},{24,16},{1,9},{9,1},{17,25},{25,17},{2,10},{10... | collective-permute-start | bytes 3538952 | tf_op jit(solution)/shard_map/ppermute | solution.py:295
  16.2 52.9 %collective-permute-start.30 = (f32[768,384]{1,0:T(8,128)}, f32[768,384]{1,0:T(8,128)}, u32[]{:S(2)}, u32[]{:S(2)}) collective-permute-start(f32[768,384]{1,0:T(8,128)} %get-tuple-element.747), channel_id=1, source_target_pairs={{0,16},{8,24},{16,0},{24,8},{1,17},{9,25},{17,1},{25,9},{2,18},{10... | collective-permute-start | bytes 3538952 | tf_op jit(solution)/shard_map/ppermute | solution.py:295
  17.9 51.3 %collective-permute-start.31 = (f32[768,384]{1,0:T(8,128)}, f32[768,384]{1,0:T(8,128)}, u32[]{:S(2)}, u32[]{:S(2)}) collective-permute-start(f32[768,384]{1,0:T(8,128)} %get-tuple-element.744), channel_id=1, source_target_pairs={{0,24},{8,16},{16,8},{24,0},{1,25},{9,17},{17,9},{25,1},{2,26},{10... | collective-permute-start | bytes 3538952 | tf_op jit(solution)/shard_map/ppermute | solution.py:295
  23.8 53.6 %collective-permute-start.32 = (f32[768,384]{1,0:T(8,128)S(1)}, f32[768,384]{1,0:T(8,128)}, u32[]{:S(2)}, u32[]{:S(2)}) collective-permute-start(f32[768,384]{1,0:T(8,128)S(1)} %get-tuple-element.1220.refs_0_), channel_id=1, source_target_pairs={{0,1},{1,0},{2,3},{3,2},{4,5},{5,4},{6,7},{7,6},{8,9},{9,8},{10,11... | collective-permute-start | bytes 3538952 | tf_op jit(solution)/shard_map/ppermute | solution.py:298
  97.4 56.9 %collective-permute-start.42 = (f32[16,128,128]{2,1,0:T(8,128)}, f32[16,128,128]{2,1,0:T(8,128)}, u32[]{:S(2)}, u32[]{:S(2)}) collective-permute-start(f32[16,128,128]{2,1,0:T(8,128)} %get-tuple-element.427.refs_1_.refs_0_), channel_id=1, source_target_pairs={{0,16},{1,9},{2,18},{3,11},{4,20},{5,13},{6,22},{7,15},{8,24},{9,1... | collective-permute-start | bytes 3145736 | tf_op jit(solution)/shard_map/ppermute | solution.py:381
  98.5 128.0 %collective-permute-start.36 = (f32[35,128,128]{2,1,0:T(8,128)}, f32[35,128,128]{2,1,0:T(8,128)S(1)}, u32[]{:S(2)}, u32[]{:S(2)}) collective-permute-start(f32[35,128,128]{2,1,0:T(8,128)} %get-tuple-element.424.refs_0_), channel_id=1, source_target_pairs={{0,2},{1,3},{2,6},{3,7},{6,4},{7,5},{4,0},{5,1},{8,10},{9,11},{10,... | collective-permute-start | bytes 6881288 | tf_op jit(solution)/shard_map/ppermute | solution.py:301
  143.3 83.1 %collective-permute-start.39 = (f32[35,128,128]{2,1,0:T(8,128)}, f32[35,128,128]{2,1,0:T(8,128)}, u32[]{:S(2)}, u32[]{:S(2)}) collective-permute-start(f32[35,128,128]{2,1,0:T(8,128)} %get-tuple-element.430), channel_id=1, source_target_pairs={{0,8},{1,17},{2,10},{3,19},{4,12},{5,21},{6,14},{7,23},{8,0},{9,25... | collective-permute-start | bytes 6881288 | tf_op jit(solution)/shard_map/ppermute | solution.py:381
  144.3 82.1 %collective-permute-start.40 = (f32[35,128,128]{2,1,0:T(8,128)}, f32[35,128,128]{2,1,0:T(8,128)}, u32[]{:S(2)}, u32[]{:S(2)}) collective-permute-start(f32[35,128,128]{2,1,0:T(8,128)} %get-tuple-element.430), channel_id=1, source_target_pairs={{0,16},{1,9},{2,18},{3,11},{4,20},{5,13},{6,22},{7,15},{8,24},{9,1... | collective-permute-start | bytes 6881288 | tf_op jit(solution)/shard_map/ppermute | solution.py:381
  180.6 43.4 %collective-permute-start.44 = (f32[32,128,128]{2,1,0:T(8,128)}, f32[32,128,128]{2,1,0:T(8,128)}, u32[]{:S(2)}, u32[]{:S(2)}) collective-permute-start(f32[32,128,128]{2,1,0:T(8,128)} %shard_map.70.refs_2_.refs_1_), channel_id=1, source_target_pairs={{0,2},{1,3},{2,6},{3,7},{6,4},{7,5},{4,0},{5,1},{8,10},{9,11},{10,... | collective-permute-start | bytes 6291464 | tf_op jit(solution)/shard_map/ppermute | solution.py:301
  224.0 49.8 %collective-permute-start.49 = (f32[32,128,128]{2,1,0:T(8,128)}, f32[32,128,128]{2,1,0:T(8,128)}, u32[]{:S(2)}, u32[]{:S(2)}) collective-permute-start(f32[32,128,128]{2,1,0:T(8,128)} %collective-permute-done.44.refs_1_.refs_2_), channel_id=1, source_target_pairs={{0,2},{1,3},{2,6},{3,7},{6,4},{7,5},{4,0},{5,1},{8,10},{9,11},{10,... | collective-permute-start | bytes 6291464 | tf_op jit(solution)/shard_map/ppermute | solution.py:301
  227.8 95.0 %collective-permute-start.41 = (f32[35,128,128]{2,1,0:T(8,128)}, f32[35,128,128]{2,1,0:T(8,128)S(1)}, u32[]{:S(2)}, u32[]{:S(2)}) collective-permute-start(f32[35,128,128]{2,1,0:T(8,128)} %get-tuple-element.431.refs_0_), channel_id=1, source_target_pairs={{0,2},{1,3},{2,6},{3,7},{6,4},{7,5},{4,0},{5,1},{8,10},{9,11},{10,... | collective-permute-start | bytes 6881288 | tf_op jit(solution)/shard_map/ppermute | solution.py:301
  227.8 95.0 %collective-permute-start.45 = (f32[35,128,128]{2,1,0:T(8,128)}, f32[35,128,128]{2,1,0:T(8,128)S(1)}, u32[]{:S(2)}, u32[]{:S(2)}) collective-permute-start(f32[35,128,128]{2,1,0:T(8,128)} %get-tuple-element.431.refs_0_), channel_id=1, source_target_pairs={{0,8},{1,17},{2,10},{3,19},{4,12},{5,21},{6,14},{7,23},{8,0},{9,25... | collective-permute-start | bytes 6881288 | tf_op jit(solution)/shard_map/ppermute | solution.py:381
  233.9 41.5 %collective-permute-start.43 = (f32[35,128,128]{2,1,0:T(8,128)}, f32[35,128,128]{2,1,0:T(8,128)S(1)}, u32[]{:S(2)}, u32[]{:S(2)}) collective-permute-start(f32[35,128,128]{2,1,0:T(8,128)} %collective-permute-done.39.refs_2_.refs_0_), channel_id=1, source_target_pairs={{0,16},{1,9},{2,18},{3,11},{4,20},{5,13},{6,22},{7,15},{8,24},{9,1... | collective-permute-start | bytes 6881288 | tf_op jit(solution)/shard_map/ppermute | solution.py:381
  269.6 53.2 %collective-permute-start.46 = (f32[35,128,128]{2,1,0:T(8,128)S(1)}, f32[35,128,128]{2,1,0:T(8,128)S(1)}, u32[]{:S(2)}, u32[]{:S(2)}) collective-permute-start(f32[35,128,128]{2,1,0:T(8,128)S(1)} %copy-done.18), channel_id=1, source_target_pairs={{0,16},{1,9},{2,18},{3,11},{4,20},{5,13},{6,22},{7,15},{8,24},{9,1... | collective-permute-start | bytes 6881288 | tf_op jit(solution)/shard_map/ppermute | solution.py:381
  273.8 230.5 %collective-permute-start.53 = (f32[32,128,128]{2,1,0:T(8,128)}, f32[32,128,128]{2,1,0:T(8,128)}, u32[]{:S(2)}, u32[]{:S(2)}) collective-permute-start(f32[32,128,128]{2,1,0:T(8,128)} %collective-permute-done.49.refs_1_.refs_2_), channel_id=1, source_target_pairs={{0,2},{1,3},{2,6},{3,7},{6,4},{7,5},{4,0},{5,1},{8,10},{9,11},{10,... | collective-permute-start | bytes 6291464 | tf_op jit(solution)/shard_map/ppermute | solution.py:301
  325.6 84.8 %collective-permute-start.47 = (f32[35,128,128]{2,1,0:T(8,128)}, f32[35,128,128]{2,1,0:T(8,128)S(1)}, u32[]{:S(2)}, u32[]{:S(2)}) collective-permute-start(f32[35,128,128]{2,1,0:T(8,128)} %get-tuple-element.439.refs_0_), channel_id=1, source_target_pairs={{0,2},{1,3},{2,6},{3,7},{6,4},{7,5},{4,0},{5,1},{8,10},{9,11},{10,... | collective-permute-start | bytes 6881288 | tf_op jit(solution)/shard_map/ppermute | solution.py:301
  327.2 83.3 %collective-permute-start.50 = (f32[35,128,128]{2,1,0:T(8,128)}, f32[35,128,128]{2,1,0:T(8,128)S(1)}, u32[]{:S(2)}, u32[]{:S(2)}) collective-permute-start(f32[35,128,128]{2,1,0:T(8,128)} %get-tuple-element.439.refs_0_), channel_id=1, source_target_pairs={{0,8},{1,17},{2,10},{3,19},{4,12},{5,21},{6,14},{7,23},{8,0},{9,25... | collective-permute-start | bytes 6881288 | tf_op jit(solution)/shard_map/ppermute | solution.py:381
  330.9 37.8 %collective-permute-start.48 = (f32[35,128,128]{2,1,0:T(8,128)}, f32[35,128,128]{2,1,0:T(8,128)S(1)}, u32[]{:S(2)}, u32[]{:S(2)}) collective-permute-start(f32[35,128,128]{2,1,0:T(8,128)} %copy-done.19), channel_id=1, source_target_pairs={{0,16},{1,9},{2,18},{3,11},{4,20},{5,13},{6,22},{7,15},{8,24},{9,1... | collective-permute-start | bytes 6881288 | tf_op jit(solution)/shard_map/ppermute | solution.py:381
  368.3 42.2 %collective-permute-start.51 = (f32[35,128,128]{2,1,0:T(8,128)S(1)}, f32[35,128,128]{2,1,0:T(8,128)S(1)}, u32[]{:S(2)}, u32[]{:S(2)}) collective-permute-start(f32[35,128,128]{2,1,0:T(8,128)S(1)} %copy-done.24), channel_id=1, source_target_pairs={{0,16},{1,9},{2,18},{3,11},{4,20},{5,13},{6,22},{7,15},{8,24},{9,1... | collective-permute-start | bytes 6881288 | tf_op jit(solution)/shard_map/ppermute | solution.py:381
  413.3 112.4 %collective-permute-start.54 = (f32[35,128,128]{2,1,0:T(8,128)}, f32[35,128,128]{2,1,0:T(8,128)S(1)}, u32[]{:S(2)}, u32[]{:S(2)}) collective-permute-start(f32[35,128,128]{2,1,0:T(8,128)} %get-tuple-element.453.refs_0_), channel_id=1, source_target_pairs={{0,8},{1,17},{2,10},{3,19},{4,12},{5,21},{6,14},{7,23},{8,0},{9,25... | collective-permute-start | bytes 6881288 | tf_op jit(solution)/shard_map/ppermute | solution.py:381
  413.3 112.4 %collective-permute-start.55 = (f32[35,128,128]{2,1,0:T(8,128)}, f32[35,128,128]{2,1,0:T(8,128)S(1)}, u32[]{:S(2)}, u32[]{:S(2)}) collective-permute-start(f32[35,128,128]{2,1,0:T(8,128)} %get-tuple-element.453.refs_0_), channel_id=1, source_target_pairs={{0,16},{1,9},{2,18},{3,11},{4,20},{5,13},{6,22},{7,15},{8,24},{9,1... | collective-permute-start | bytes 6881288 | tf_op jit(solution)/shard_map/ppermute | solution.py:381
  413.3 72.5 %collective-permute-start.52 = (f32[35,128,128]{2,1,0:T(8,128)}, f32[35,128,128]{2,1,0:T(8,128)S(1)}, u32[]{:S(2)}, u32[]{:S(2)}) collective-permute-start(f32[35,128,128]{2,1,0:T(8,128)} %copy-done.21), channel_id=1, source_target_pairs={{0,16},{1,9},{2,18},{3,11},{4,20},{5,13},{6,22},{7,15},{8,24},{9,1... | collective-permute-start | bytes 6881288 | tf_op jit(solution)/shard_map/ppermute | solution.py:381
  522.9 37.3 %collective-permute-start.56 = (f32[512,768]{1,0:T(8,128)S(1)}, f32[512,768]{1,0:T(8,128)S(1)}, u32[]{:S(2)}, u32[]{:S(2)}) collective-permute-start(f32[512,768]{1,0:T(8,128)S(1)} %slice.1317), channel_id=1, source_target_pairs={{0,1},{1,0},{2,3},{3,2},{4,5},{5,4},{6,7},{7,6},{8,9},{9,8},{10,11... | collective-permute-start | bytes 4718600 | tf_op jit(solution)/shard_map/ppermute | solution.py:298
  525.7 39.6 %collective-permute-start.57 = (f32[35,128,128]{2,1,0:T(8,128)S(1)}, f32[35,128,128]{2,1,0:T(8,128)S(1)}, u32[]{:S(2)}, u32[]{:S(2)}) collective-permute-start(f32[35,128,128]{2,1,0:T(8,128)S(1)} %collective-permute-done.54.refs_0_), channel_id=1, source_target_pairs={{0,16},{1,9},{2,18},{3,11},{4,20},{5,13},{6,22},{7,15},{8,24},{9,1... | collective-permute-start | bytes 6881288 | tf_op jit(solution)/shard_map/ppermute | solution.py:381
  (55 other events, 647.6 us)
